TPU v7x, 32 devices: a whole 2x2x4 slice. The times are simulated.
32 devices in a mesh: focus: 2 (over y), tx: 4 (over z), ty: 2 (over core), dose: 2 (over x).
Axes of the slice: x: 2, y: 2, z: 4, core: 2. Of those that a mesh axis runs over, the one named last changes fastest.
Arguments:
- aerial_image: float32 [64, 32, 256], P('focus', 'tx', 'ty'), parts along dimension 0, may hold values from 0.2 to 2
- quencher: float32 [32, 32, 256], P(None, 'tx', 'ty'), may hold values from 0.1 to 0.8
- cotangent: float32 [8, 32, 32, 256], P(('focus', 'dose'), None, 'tx', 'ty'), parts along dimension 0, may hold values from -6 to 6
- dose_levels: float32 [16], replicated, may hold values from 0.5 to 2
- dose_index: int32 [8], P(('focus', 'dose')), parts along dimension 0, may hold values from 0 to 15
Outputs:
- image_grad: float32 [64, 32, 256], P(('focus', 'dose'), 'tx', 'ty'), parts along dimension 0
There are 2 independent parts, one for each index of `focus`. A program takes and returns all parts, laid end to end along the dimension named above; an argument that names none is the same for every part. Nothing has to cross between parts.
All inputs are finite; a program needn't handle non-finite values.
Results may differ from a plain program's by a relative error of at most 0.00002.
Values sent between devices are 32-bit elements; how exact they have to be, the bound alone decides.
A program may use at most 64 MiB of HBM per device.

v0:
```python
import jax
import jax.numpy as jnp
from jax import lax
from jax.sharding import PartitionSpec as P

STEPS = 4


exposure_rate = 1.0
neutral_rate = 0.8
deprotect_rate = 0.5
acid_lateral = 0.23
acid_depth = 0.02
base_lateral = 0.2
base_depth = 0.02


def with_halo(value, sides, width):
    for axis, dim in sides:
        devices, length = (lax.axis_size(axis), value.shape[dim])
        up = [(i, (i + 1) % devices) for i in range(devices)]
        down = [(j, i) for i, j in up]
        last = lax.slice_in_dim(value, length - width, length, axis=dim)
        leading = lax.slice_in_dim(value, 0, width, axis=dim)
        before = lax.ppermute(last, axis, up)
        after = lax.ppermute(leading, axis, down)
        value = jnp.concatenate([before, value, after], axis=dim)
    return value


def shrink(field):
    return field[..., 1:-1, 1:-1]


def diffuse(padded):
    center = shrink(padded)
    lateral = (
        padded[..., 2:, 1:-1]
        + padded[..., :-2, 1:-1]
        + padded[..., 1:-1, 2:]
        + padded[..., 1:-1, :-2]
        - 4.0 * center
    )
    upward = jnp.concatenate((center[..., 1:, :, :], center[..., -1:, :, :]), axis=-3)
    downward = jnp.concatenate((center[..., :1, :, :], center[..., :-1, :, :]), axis=-3)
    return (lateral, upward + downward - 2.0 * center)


def advance(padded, protect):
    center = shrink(padded)
    acid_now = center[:, 0]
    quench_now = center[:, 1]
    reaction = neutral_rate * acid_now * quench_now
    lateral, vertical = diffuse(padded)
    next_acid = acid_now + acid_lateral * lateral[:, 0] + acid_depth * vertical[:, 0] - reaction
    next_quench = quench_now + base_lateral * lateral[:, 1] + base_depth * vertical[:, 1] - reaction
    snapshot = jnp.concatenate((center, protect[:, None]), axis=1)
    next_protect = protect * (1.0 - deprotect_rate * acid_now)
    return (jnp.stack((next_acid, next_quench), axis=1), next_protect, snapshot)


def retreat(padded, adj_protect, snapshot):
    center = shrink(padded)
    adj_acid = center[:, 0]
    adj_quench = center[:, 1]
    acid_old = snapshot[:, 0]
    quench_old = snapshot[:, 1]
    protect_old = snapshot[:, 2]
    lateral, vertical = diffuse(padded)
    adj_sum = adj_acid + adj_quench
    next_acid = (
        adj_acid
        + acid_lateral * lateral[:, 0]
        + acid_depth * vertical[:, 0]
        - neutral_rate * quench_old * adj_sum
        - deprotect_rate * protect_old * adj_protect
    )
    next_quench = (
        adj_quench
        + base_lateral * lateral[:, 1]
        + base_depth * vertical[:, 1]
        - neutral_rate * acid_old * adj_sum
    )
    next_protect = adj_protect * (1.0 - deprotect_rate * acid_old)
    return (jnp.stack((next_acid, next_quench), axis=1), next_protect)


def on_device(aerial_image, quencher, cotangent, dose_levels, dose_index):
    levels = jnp.arange(dose_levels.shape[0], dtype=jnp.int32)
    choose_mask = (dose_index[:, None] == levels[None, :]).astype(jnp.float32)
    dose_value = jnp.sum(choose_mask * dose_levels[None, :], axis=1)
    dose_col = dose_value[:, None, None, None]
    absorbed = jnp.exp(-exposure_rate * dose_col * aerial_image[None])
    acid_now = 1.0 - absorbed
    quench_now = jnp.broadcast_to(quencher[None], acid_now.shape)
    fields = jnp.stack((acid_now, quench_now), axis=1)
    protect = jnp.ones_like(acid_now)
    history = []
    for bake_step in range(STEPS):
        padded = with_halo(fields, (("tx", 3), ("ty", 4)), 1)
        fields, protect, snapshot = advance(padded, protect)
        history.append(snapshot)
    adjoint = jnp.zeros_like(fields)
    adj_protect = cotangent
    for bake_step in reversed(range(STEPS)):
        padded = with_halo(adjoint, (("tx", 3), ("ty", 4)), 1)
        adjoint, adj_protect = retreat(padded, adj_protect, history[bake_step])
    partial_value = jnp.sum(adjoint[:, 0] * exposure_rate * dose_col * absorbed, axis=0)
    return lax.psum_scatter(partial_value, "dose", scatter_dimension=0, tiled=True)


def solution(mesh):
    placed = (
        P("focus", "tx", "ty"),
        P(None, "tx", "ty"),
        P(("focus", "dose"), None, "tx", "ty"),
        P(),
        P(("focus", "dose")),
    )
    return jax.shard_map(
        on_device,
        mesh=mesh,
        in_specs=placed,
        out_specs=P(("focus", "dose"), "tx", "ty"),
        check_vma=False,
    )
```

profile of v0, /device:TPU:0, one launch (start us, length us, event | category | flops | bytes accessed | tf_op | source)
XLA Modules:
  0.0 161.6 jit_solution(10039179641620063067)
XLA Ops:
  7.3 5.0 %collective-permute-start = (f32[2,2,32,1,128]{2,1,4,3,0:T(2,128)}, f32[2,2,32,1,128]{2,1,4,3,0:T(2,128)S(1)}, u32[]{:S(2)}, u32[]{:S(2)}) collective-permute-start(f32[2,2,32,1,128]{2,1,4,3,0:T(2,128)} %broadcast.202), channel_id=1, source_target_pairs={{4,0},{8,4},{12,8},{0,12},{5,1},{9,5},{13,9},{1,13},{6,2},{10,6},{... | collective-permute-start | bytes 196616 | tf_op jit(solution)/shard_map/ppermute | solution.py:26
  16.9 3.8 %collective-permute-start.4 = (f32[2,2,32,1,128]{2,4,3,0,1:T(8,128)}, f32[2,2,32,1,128]{2,4,3,0,1:T(8,128)}, u32[]{:S(2)}, u32[]{:S(2)}) collective-permute-start(f32[2,2,32,1,128]{2,4,3,0,1:T(8,128)} %get-tuple-element.69), channel_id=1, source_target_pairs={{4,0},{8,4},{12,8},{0,12},{5,1},{9,5},{13,9},{1,13},{6,2},{10,6},{... | collective-permute-start | bytes 196616 | tf_op jit(solution)/shard_map/ppermute | solution.py:26
  20.7 2.8 %fusion.29 = (f32[2,2,1,8,128]{2,4,3,0,1:T(8,128)}, f32[2,2,1,8,128]{2,4,3,0,1:T(8,128)}) fusion(f32[2,1,32,8,128]{2,4,3,0,1:T(8,128)S(1)} %exponential_subtract_fusion, f32[2,1,32,8,128]{2,4,3,0,1:T(8,128)S(1)} %stack_broadcast_in_dim.2), kind=kLoop, calls=%fused_computation.110 | loop fusion | flops 8192 | bytes 557056 | tf_op jit(solution)/shard_map/stack | solution.py:96
  23.4 2.8 %fusion.30 = (f32[2,2,31,8,128]{2,4,3,0,1:T(8,128)}, f32[2,2,31,8,128]{2,4,3,0,1:T(8,128)}) fusion(f32[2,1,32,8,128]{2,4,3,0,1:T(8,128)S(1)} %exponential_subtract_fusion, f32[2,1,32,8,128]{2,4,3,0,1:T(8,128)S(1)} %stack_broadcast_in_dim.2), kind=kLoop, calls=%fused_computation.111 | loop fusion | flops 253952 | bytes 1540096 | tf_op jit(solution)/shard_map/stack | solution.py:96
  27.3 1.3 copy.429
  28.6 4.6 %fusion.2 = f32[2,2,32,8,128]{2,4,3,0,1:T(8,128)S(1)} fusion(f32[2,1,32,8,128]{2,4,3,0,1:T(8,128)S(1)} %stack_broadcast_in_dim.2, f32[2,1,32,8,128]{2,4,3,0,1:T(8,128)S(1)} %exponential_subtract_fusion, f32[2,2,1,8,128]{2,4,3,0,1:T(8,128)} %get-tuple-element.65, f32[2,2,31,8,128]{2,4,3,0,1:T(8,128)} %get-tuple-element.67, ...), kind=kLoop, calls=%fused_computation.83 | loop fusion | flops 786432 | bytes 2097152 | tf_op jit(solution)/shard_map/sub | solution.py:46
  33.2 2.8 %collective-permute-done.5 = f32[2,2,32,1,128]{2,4,3,0,1:T(8,128)} collective-permute-done((f32[2,2,32,1,128]{2,4,3,0,1:T(8,128)}, f32[2,2,32,1,128]{2,4,3,0,1:T(8,128)}, u32[]{:S(2)}, u32[]{:S(2)}) %collective-permute-start.5) | collective-permute-done | bytes 65568 | tf_op jit(solution)/shard_map/ppermute | solution.py:25
  39.7 2.4 %fusion.3 = f32[2,2,32,8,128]{2,4,3,0,1:T(8,128)S(1)} fusion(f32[2,1,32,8,128]{2,4,3,0,1:T(8,128)S(1)} %stack_broadcast_in_dim.2, f32[2,1,32,8,128]{2,4,3,0,1:T(8,128)S(1)} %exponential_subtract_fusion, f32[2,2,32,10,1]{2,4,3,0,1:T(1,128)S(1)} %copy.417, f32[2,2,32,1,128]{2,4,3,0,1:T(8,128)} %collective-permute-done.4, ...), kind=kLoop, calls=%fused_computation.84 | loop fusion | flops 2359296 | bytes 1189888 | tf_op jit(solution)/shard_map/sub | solution.py:38
  43.7 1.8 %collective-permute-start.8 = (f32[2,2,32,1,128]{2,4,3,0,1:T(8,128)S(1)}, f32[2,2,32,1,128]{2,4,3,0,1:T(8,128)S(1)}, u32[]{:S(2)}, u32[]{:S(2)}) collective-permute-start(f32[2,2,32,1,128]{2,4,3,0,1:T(8,128)S(1)} %get-tuple-element.63), channel_id=1, source_target_pairs={{4,0},{8,4},{12,8},{0,12},{5,1},{9,5},{13,9},{1,13},{6,2},{10,6},{... | collective-permute-start | bytes 196616 | tf_op jit(solution)/shard_map/ppermute | solution.py:26
  45.8 4.5 %fusion.6 = f32[2,2,32,8,128]{2,1,4,3,0:T(2,128)S(1)} fusion(f32[2,2,32,1,128]{2,1,4,3,0:T(2,128)S(1)} %collective-permute-done, f32[2,2,32,1,128]{2,1,4,3,0:T(2,128)} %collective-permute-done.1, f32[2,2,32,10,1]{2,1,4,3,0:T(2,128)S(1)} %collective-permute-done.3, f32[2,2,32,8,128]{2,1,4,3,0:T(2,128)S(1)} %broadcast_in_dim.2, ...), kind=kLoop, calls=%fused_computation.87 | loop fusion | flops 1179648 | bytes 1189888 | tf_op jit(solution)/shard_map/add | solution.py:38
  50.4 2.2 %slice_multiply_fusion.10 = (f32[2,1,32,8,128]{2,1,4,3,0:T(1,128)S(1)}, f32[2,1,32,8,128]{2,1,4,3,0:T(1,128)S(1)}) fusion(f32[2,1,32,8,128]{2,1,4,3,0:T(1,128)S(1)} %bitcast.187, f32[2,2,32,8,128]{2,1,4,3,0:T(2,128)S(1)} %fusion.6), kind=kLoop, calls=%fused_computation.274 | loop fusion | flops 65536 | bytes 1310720 | tf_op jit(solution)/shard_map/mul | solution.py:80
  53.4 4.5 %collective-permute-done.9 = f32[2,2,32,1,128]{2,4,3,0,1:T(8,128)S(1)} collective-permute-done((f32[2,2,32,1,128]{2,4,3,0,1:T(8,128)S(1)}, f32[2,2,32,1,128]{2,4,3,0,1:T(8,128)S(1)}, u32[]{:S(2)}, u32[]{:S(2)}) %collective-permute-start.9) | collective-permute-done | bytes 65568 | tf_op jit(solution)/shard_map/ppermute | solution.py:25
  59.9 1.3 fusion.44
  62.7 2.3 %collective-permute-start.12 = (f32[2,2,32,1,128]{2,4,3,0,1:T(8,128)S(1)}, f32[2,2,32,1,128]{2,4,3,0,1:T(8,128)S(1)}, u32[]{:S(2)}, u32[]{:S(2)}) collective-permute-start(f32[2,2,32,1,128]{2,4,3,0,1:T(8,128)S(1)} %get-tuple-element.53), channel_id=1, source_target_pairs={{4,0},{8,4},{12,8},{0,12},{5,1},{9,5},{13,9},{1,13},{6,2},{10,6},{... | collective-permute-start | bytes 196616 | tf_op jit(solution)/shard_map/ppermute | solution.py:26
  65.8 5.9 %collective-permute-done.12 = f32[2,2,32,1,128]{2,4,3,0,1:T(8,128)S(1)} collective-permute-done((f32[2,2,32,1,128]{2,4,3,0,1:T(8,128)S(1)}, f32[2,2,32,1,128]{2,4,3,0,1:T(8,128)S(1)}, u32[]{:S(2)}, u32[]{:S(2)}) %collective-permute-start.12) | collective-permute-done | bytes 65568 | tf_op jit(solution)/shard_map/ppermute | solution.py:26
  71.7 6.6 %collective-permute-done.13 = f32[2,2,32,1,128]{2,4,3,0,1:T(8,128)S(1)} collective-permute-done((f32[2,2,32,1,128]{2,4,3,0,1:T(8,128)S(1)}, f32[2,2,32,1,128]{2,4,3,0,1:T(8,128)S(1)}, u32[]{:S(2)}, u32[]{:S(2)}) %collective-permute-start.13) | collective-permute-done | bytes 65568 | tf_op jit(solution)/shard_map/ppermute | solution.py:25
  80.3 1.3 fusion.40
  82.2 2.0 %fusion.104 = (f32[2,32,8,128]{1,3,2,0:T(8,128)S(1)}, f32[2,32,8,128]{1,3,2,0:T(8,128)S(1)}, f32[2,32,8,128]{1,3,2,0:T(8,128)S(1)}, f32[2,32,8,128]{1,3,2,0:T(8,128)S(1)}, f32[2,32,8,128]{1,3,2,0:T(8,128)S(1)}) fusion(f32[2,2,32,8,128]{2,4,3,0,1:T(8,128)S(1)} %fusion.51, f32[2,2,32,8,128]{2,4,3,0,1:T(8,128)S(1)} %fusion.40, ...), kind=kLoop, calls=%fused_computation.281 | loop fusion | flops 3080192 | bytes 4849800 | tf_op jit(solution)/shard_map/sub | solution.py:72
  85.0 1.8 %collective-permute-start.16 = (f32[2,2,32,1,128]{2,4,3,0,1:T(8,128)S(1)}, f32[2,2,32,1,128]{2,4,3,0,1:T(8,128)S(1)}, u32[]{:S(2)}, u32[]{:S(2)}) collective-permute-start(f32[2,2,32,1,128]{2,4,3,0,1:T(8,128)S(1)} %get-tuple-element.45), channel_id=1, source_target_pairs={{4,0},{8,4},{12,8},{0,12},{5,1},{9,5},{13,9},{1,13},{6,2},{10,6},{... | collective-permute-start | bytes 196616 | tf_op jit(solution)/shard_map/ppermute | solution.py:26
  87.9 6.0 %collective-permute-done.16 = f32[2,2,32,1,128]{2,4,3,0,1:T(8,128)S(1)} collective-permute-done((f32[2,2,32,1,128]{2,4,3,0,1:T(8,128)S(1)}, f32[2,2,32,1,128]{2,4,3,0,1:T(8,128)S(1)}, u32[]{:S(2)}, u32[]{:S(2)}) %collective-permute-start.16) | collective-permute-done | bytes 65568 | tf_op jit(solution)/shard_map/ppermute | solution.py:26
  93.9 5.4 %collective-permute-done.17 = f32[2,2,32,1,128]{2,4,3,0,1:T(8,128)S(1)} collective-permute-done((f32[2,2,32,1,128]{2,4,3,0,1:T(8,128)S(1)}, f32[2,2,32,1,128]{2,4,3,0,1:T(8,128)S(1)}, u32[]{:S(2)}, u32[]{:S(2)}) %collective-permute-start.17) | collective-permute-done | bytes 65568 | tf_op jit(solution)/shard_map/ppermute | solution.py:25
  101.2 1.3 fusion.36
  105.4 1.8 %collective-permute-start.20 = (f32[2,2,32,1,128]{2,4,3,0,1:T(8,128)S(1)}, f32[2,2,32,1,128]{2,4,3,0,1:T(8,128)S(1)}, u32[]{:S(2)}, u32[]{:S(2)}) collective-permute-start(f32[2,2,32,1,128]{2,4,3,0,1:T(8,128)S(1)} %get-tuple-element.39), channel_id=1, source_target_pairs={{4,0},{8,4},{12,8},{0,12},{5,1},{9,5},{13,9},{1,13},{6,2},{10,6},{... | collective-permute-start | bytes 196616 | tf_op jit(solution)/shard_map/ppermute | solution.py:26
  108.3 5.6 %collective-permute-done.20 = f32[2,2,32,1,128]{2,4,3,0,1:T(8,128)S(1)} collective-permute-done((f32[2,2,32,1,128]{2,4,3,0,1:T(8,128)S(1)}, f32[2,2,32,1,128]{2,4,3,0,1:T(8,128)S(1)}, u32[]{:S(2)}, u32[]{:S(2)}) %collective-permute-start.20) | collective-permute-done | bytes 65568 | tf_op jit(solution)/shard_map/ppermute | solution.py:26
  113.9 6.3 %collective-permute-done.21 = f32[2,2,32,1,128]{2,4,3,0,1:T(8,128)S(1)} collective-permute-done((f32[2,2,32,1,128]{2,4,3,0,1:T(8,128)S(1)}, f32[2,2,32,1,128]{2,4,3,0,1:T(8,128)S(1)}, u32[]{:S(2)}, u32[]{:S(2)}) %collective-permute-start.21) | collective-permute-done | bytes 65568 | tf_op jit(solution)/shard_map/ppermute | solution.py:25
  122.2 1.3 fusion.32
  123.5 1.5 fusion.79
  125.1 1.7 %collective-permute-start.24 = (f32[2,2,32,1,128]{2,4,3,0,1:T(8,128)S(1)}, f32[2,2,32,1,128]{2,4,3,0,1:T(8,128)S(1)}, u32[]{:S(2)}, u32[]{:S(2)}) collective-permute-start(f32[2,2,32,1,128]{2,4,3,0,1:T(8,128)S(1)} %get-tuple-element.33), channel_id=1, source_target_pairs={{4,0},{8,4},{12,8},{0,12},{5,1},{9,5},{13,9},{1,13},{6,2},{10,6},{... | collective-permute-start | bytes 196616 | tf_op jit(solution)/shard_map/ppermute | solution.py:26
  127.9 5.6 %collective-permute-done.24 = f32[2,2,32,1,128]{2,4,3,0,1:T(8,128)S(1)} collective-permute-done((f32[2,2,32,1,128]{2,4,3,0,1:T(8,128)S(1)}, f32[2,2,32,1,128]{2,4,3,0,1:T(8,128)S(1)}, u32[]{:S(2)}, u32[]{:S(2)}) %collective-permute-start.24) | collective-permute-done | bytes 65568 | tf_op jit(solution)/shard_map/ppermute | solution.py:26
  133.5 6.6 %collective-permute-done.25 = f32[2,2,32,1,128]{2,4,3,0,1:T(8,128)S(1)} collective-permute-done((f32[2,2,32,1,128]{2,4,3,0,1:T(8,128)S(1)}, f32[2,2,32,1,128]{2,4,3,0,1:T(8,128)S(1)}, u32[]{:S(2)}, u32[]{:S(2)}) %collective-permute-start.25) | collective-permute-done | bytes 65568 | tf_op jit(solution)/shard_map/ppermute | solution.py:25
  141.7 2.3 %fusion.115 = f32[32,8,128]{0,2,1:T(8,128)S(1)} fusion(f32[2,32,8,128]{1,3,2,0:T(8,128)S(1)} %get-tuple-element.13, f32[2,32,8,128]{1,3,2,0:T(8,128)S(1)} %get-tuple-element.12, f32[2,1,32,8,128]{2,4,3,0,1:T(8,128)S(1)} %bitcast.177, f32[2,1,32,8,128]{2,4,3,0,1:T(8,128)S(1)} %bitcast.182, f32[2,2,31,8,128]{2,4,3,0,1:T(8,128)S(1)} %get-tuple-element.35, ...), kind=kLoop, calls=%fused_computation.325 | loop fusion | flops 2981888 | bytes 3680272 | tf_op jit(solution)/shard_map/reduce_sum | solution.py:108
  144.9 9.8 %reduce-scatter.2.cloned.1.call-done = f32[16,8,128]{2,1,0:T(8,128)} async-done(((f32[32,8,128]{2,1,0:T(8,128)}), f32[16,8,128]{2,1,0:T(8,128)}) %reduce-scatter.2.cloned.1.call-update) | async-done | bytes 65552 | tf_op jit(solution)/shard_map/reduce_scatter | solution.py:109
  (123 shorter events, 32.4 us)
Async XLA Ops:
  6.5 148.2 %reduce-scatter.2.cloned.1.call-start = ((), (), s32[]{:S(2)}) async-start(), calls=%async_computation.1 | async-start | bytes 196608 | tf_op jit(solution)/shard_map/reduce_scatter | solution.py:109
  7.3 30.2 %collective-permute-start = (f32[2,2,32,1,128]{2,1,4,3,0:T(2,128)}, f32[2,2,32,1,128]{2,1,4,3,0:T(2,128)S(1)}, u32[]{:S(2)}, u32[]{:S(2)}) collective-permute-start(f32[2,2,32,1,128]{2,1,4,3,0:T(2,128)} %broadcast.202), channel_id=1, source_target_pairs={{4,0},{8,4},{12,8},{0,12},{5,1},{9,5},{13,9},{1,13},{6,2},{10,6},{... | collective-permute-start | bytes 196616 | tf_op jit(solution)/shard_map/ppermute | solution.py:26
  12.4 25.2 %collective-permute-start.1 = (f32[2,2,32,1,128]{2,1,4,3,0:T(2,128)}, f32[2,2,32,1,128]{2,1,4,3,0:T(2,128)}, u32[]{:S(2)}, u32[]{:S(2)}) collective-permute-start(f32[2,2,32,1,128]{2,1,4,3,0:T(2,128)} %broadcast.202), channel_id=1, source_target_pairs={{0,4},{4,8},{8,12},{12,0},{1,5},{5,9},{9,13},{13,1},{2,6},{6,10},{... | collective-permute-start | bytes 196616 | tf_op jit(solution)/shard_map/ppermute | solution.py:25
  13.5 3.4 %copy-start.3 = (f32[32,8,128]{0,2,1:T(8,128)}, f32[32,8,128]{0,2,1:T(8,128)S(1)}, u32[]{:S(2)}) copy-start(f32[32,8,128]{0,2,1:T(8,128)S(1)} %copy.411) | copy-start | bytes 393220
  16.9 16.4 %collective-permute-start.4 = (f32[2,2,32,1,128]{2,4,3,0,1:T(8,128)}, f32[2,2,32,1,128]{2,4,3,0,1:T(8,128)}, u32[]{:S(2)}, u32[]{:S(2)}) collective-permute-start(f32[2,2,32,1,128]{2,4,3,0,1:T(8,128)} %get-tuple-element.69), channel_id=1, source_target_pairs={{4,0},{8,4},{12,8},{0,12},{5,1},{9,5},{13,9},{1,13},{6,2},{10,6},{... | collective-permute-start | bytes 196616 | tf_op jit(solution)/shard_map/ppermute | solution.py:26
  20.7 15.4 %collective-permute-start.5 = (f32[2,2,32,1,128]{2,4,3,0,1:T(8,128)}, f32[2,2,32,1,128]{2,4,3,0,1:T(8,128)}, u32[]{:S(2)}, u32[]{:S(2)}) collective-permute-start(f32[2,2,32,1,128]{2,4,3,0,1:T(8,128)} %get-tuple-element.68), channel_id=1, source_target_pairs={{0,4},{4,8},{8,12},{12,0},{1,5},{5,9},{9,13},{13,1},{2,6},{6,10},{... | collective-permute-start | bytes 196616 | tf_op jit(solution)/shard_map/ppermute | solution.py:25
  23.4 2.8 %copy-start.5 = (f32[32,8,128]{2,1,0:T(8,128)S(1)}, f32[32,8,128]{2,1,0:T(8,128)}, u32[]{:S(2)}) copy-start(f32[32,8,128]{2,1,0:T(8,128)} %param.6) | copy-start | bytes 393220
  36.9 2.7 %collective-permute-start.7 = (f32[2,2,32,10,1]{2,1,4,3,0:T(2,128)S(1)}, f32[2,2,32,10,1]{2,1,4,3,0:T(2,128)S(1)}, u32[]{:S(2)}, u32[]{:S(2)}) collective-permute-start(f32[2,2,32,10,1]{2,1,4,3,0:T(2,128)S(1)} %copy.416), channel_id=1, source_target_pairs={{0,2},{2,0},{1,3},{3,1},{4,6},{6,4},{5,7},{7,5},{8,10},{10,8},{9,1... | collective-permute-start | bytes 15368 | tf_op jit(solution)/shard_map/ppermute | solution.py:25
  37.0 2.7 %collective-permute-start.6 = (f32[2,2,32,10,1]{2,1,4,3,0:T(2,128)S(1)}, f32[2,2,32,10,1]{2,1,4,3,0:T(2,128)S(1)}, u32[]{:S(2)}, u32[]{:S(2)}) collective-permute-start(f32[2,2,32,10,1]{2,1,4,3,0:T(2,128)S(1)} %copy.414), channel_id=1, source_target_pairs={{2,0},{0,2},{3,1},{1,3},{6,4},{4,6},{7,5},{5,7},{10,8},{8,10},{11,... | collective-permute-start | bytes 15368 | tf_op jit(solution)/shard_map/ppermute | solution.py:26
  39.0 6.8 %collective-permute-start.3 = (f32[2,2,32,10,1]{2,1,4,3,0:T(2,128)S(1)}, f32[2,2,32,10,1]{2,1,4,3,0:T(2,128)S(1)}, u32[]{:S(2)}, u32[]{:S(2)}) collective-permute-start(f32[2,2,32,10,1]{2,1,4,3,0:T(2,128)S(1)} %get-tuple-element.25), channel_id=1, source_target_pairs={{0,2},{2,0},{1,3},{3,1},{4,6},{6,4},{5,7},{7,5},{8,10},{10,8},{9,1... | collective-permute-start | bytes 15368 | tf_op jit(solution)/shard_map/ppermute | solution.py:25
  39.1 6.7 %collective-permute-start.2 = (f32[2,2,32,10,1]{2,1,4,3,0:T(2,128)S(1)}, f32[2,2,32,10,1]{2,1,4,3,0:T(2,128)S(1)}, u32[]{:S(2)}, u32[]{:S(2)}) collective-permute-start(f32[2,2,32,10,1]{2,1,4,3,0:T(2,128)S(1)} %get-tuple-element.24), channel_id=1, source_target_pairs={{2,0},{0,2},{3,1},{1,3},{6,4},{4,6},{7,5},{5,7},{10,8},{8,10},{11,... | collective-permute-start | bytes 15368 | tf_op jit(solution)/shard_map/ppermute | solution.py:26
  39.7 2.5 %copy-start.1 = (f32[32,8,128]{0,2,1:T(8,128)S(1)}, f32[32,8,128]{0,2,1:T(8,128)}, u32[]{:S(2)}) copy-start(f32[32,8,128]{0,2,1:T(8,128)} %copy-done) | copy-start | bytes 393220
  43.7 9.7 %collective-permute-start.8 = (f32[2,2,32,1,128]{2,4,3,0,1:T(8,128)S(1)}, f32[2,2,32,1,128]{2,4,3,0,1:T(8,128)S(1)}, u32[]{:S(2)}, u32[]{:S(2)}) collective-permute-start(f32[2,2,32,1,128]{2,4,3,0,1:T(8,128)S(1)} %get-tuple-element.63), channel_id=1, source_target_pairs={{4,0},{8,4},{12,8},{0,12},{5,1},{9,5},{13,9},{1,13},{6,2},{10,6},{... | collective-permute-start | bytes 196616 | tf_op jit(solution)/shard_map/ppermute | solution.py:26
  45.5 12.4 %collective-permute-start.9 = (f32[2,2,32,1,128]{2,4,3,0,1:T(8,128)S(1)}, f32[2,2,32,1,128]{2,4,3,0,1:T(8,128)S(1)}, u32[]{:S(2)}, u32[]{:S(2)}) collective-permute-start(f32[2,2,32,1,128]{2,4,3,0,1:T(8,128)S(1)} %get-tuple-element.62), channel_id=1, source_target_pairs={{0,4},{4,8},{8,12},{12,0},{1,5},{5,9},{9,13},{13,1},{2,6},{6,10},{... | collective-permute-start | bytes 196616 | tf_op jit(solution)/shard_map/ppermute | solution.py:25
  58.0 1.8 %collective-permute-start.11 = (f32[2,2,32,10,1]{2,1,4,3,0:T(2,128)S(1)}, f32[2,2,32,10,1]{2,1,4,3,0:T(2,128)S(1)}, u32[]{:S(2)}, u32[]{:S(2)}) collective-permute-start(f32[2,2,32,10,1]{2,1,4,3,0:T(2,128)S(1)} %copy.423), channel_id=1, source_target_pairs={{0,2},{2,0},{1,3},{3,1},{4,6},{6,4},{5,7},{7,5},{8,10},{10,8},{9,1... | collective-permute-start | bytes 15368 | tf_op jit(solution)/shard_map/ppermute | solution.py:25
  58.1 1.8 %collective-permute-start.10 = (f32[2,2,32,10,1]{2,1,4,3,0:T(2,128)S(1)}, f32[2,2,32,10,1]{2,1,4,3,0:T(2,128)S(1)}, u32[]{:S(2)}, u32[]{:S(2)}) collective-permute-start(f32[2,2,32,10,1]{2,1,4,3,0:T(2,128)S(1)} %copy.421), channel_id=1, source_target_pairs={{2,0},{0,2},{3,1},{1,3},{6,4},{4,6},{7,5},{5,7},{10,8},{8,10},{11,... | collective-permute-start | bytes 15368 | tf_op jit(solution)/shard_map/ppermute | solution.py:26
  62.7 9.1 %collective-permute-start.12 = (f32[2,2,32,1,128]{2,4,3,0,1:T(8,128)S(1)}, f32[2,2,32,1,128]{2,4,3,0,1:T(8,128)S(1)}, u32[]{:S(2)}, u32[]{:S(2)}) collective-permute-start(f32[2,2,32,1,128]{2,4,3,0,1:T(8,128)S(1)} %get-tuple-element.53), channel_id=1, source_target_pairs={{4,0},{8,4},{12,8},{0,12},{5,1},{9,5},{13,9},{1,13},{6,2},{10,6},{... | collective-permute-start | bytes 196616 | tf_op jit(solution)/shard_map/ppermute | solution.py:26
  65.0 13.4 %collective-permute-start.13 = (f32[2,2,32,1,128]{2,4,3,0,1:T(8,128)S(1)}, f32[2,2,32,1,128]{2,4,3,0,1:T(8,128)S(1)}, u32[]{:S(2)}, u32[]{:S(2)}) collective-permute-start(f32[2,2,32,1,128]{2,4,3,0,1:T(8,128)S(1)} %get-tuple-element.52), channel_id=1, source_target_pairs={{0,4},{4,8},{8,12},{12,0},{1,5},{5,9},{9,13},{13,1},{2,6},{6,10},{... | collective-permute-start | bytes 196616 | tf_op jit(solution)/shard_map/ppermute | solution.py:25
  78.4 1.8 %collective-permute-start.15 = (f32[2,2,32,10,1]{2,1,4,3,0:T(2,128)S(1)}, f32[2,2,32,10,1]{2,1,4,3,0:T(2,128)S(1)}, u32[]{:S(2)}, u32[]{:S(2)}) collective-permute-start(f32[2,2,32,10,1]{2,1,4,3,0:T(2,128)S(1)} %copy.427), channel_id=1, source_target_pairs={{0,2},{2,0},{1,3},{3,1},{4,6},{6,4},{5,7},{7,5},{8,10},{10,8},{9,1... | collective-permute-start | bytes 15368 | tf_op jit(solution)/shard_map/ppermute | solution.py:25
  78.5 1.8 %collective-permute-start.14 = (f32[2,2,32,10,1]{2,1,4,3,0:T(2,128)S(1)}, f32[2,2,32,10,1]{2,1,4,3,0:T(2,128)S(1)}, u32[]{:S(2)}, u32[]{:S(2)}) collective-permute-start(f32[2,2,32,10,1]{2,1,4,3,0:T(2,128)S(1)} %copy.425), channel_id=1, source_target_pairs={{2,0},{0,2},{3,1},{1,3},{6,4},{4,6},{7,5},{5,7},{10,8},{8,10},{11,... | collective-permute-start | bytes 15368 | tf_op jit(solution)/shard_map/ppermute | solution.py:26
  85.0 8.9 %collective-permute-start.16 = (f32[2,2,32,1,128]{2,4,3,0,1:T(8,128)S(1)}, f32[2,2,32,1,128]{2,4,3,0,1:T(8,128)S(1)}, u32[]{:S(2)}, u32[]{:S(2)}) collective-permute-start(f32[2,2,32,1,128]{2,4,3,0,1:T(8,128)S(1)} %get-tuple-element.45), channel_id=1, source_target_pairs={{4,0},{8,4},{12,8},{0,12},{5,1},{9,5},{13,9},{1,13},{6,2},{10,6},{... | collective-permute-start | bytes 196616 | tf_op jit(solution)/shard_map/ppermute | solution.py:26
  86.8 12.4 %collective-permute-start.17 = (f32[2,2,32,1,128]{2,4,3,0,1:T(8,128)S(1)}, f32[2,2,32,1,128]{2,4,3,0,1:T(8,128)S(1)}, u32[]{:S(2)}, u32[]{:S(2)}) collective-permute-start(f32[2,2,32,1,128]{2,4,3,0,1:T(8,128)S(1)} %get-tuple-element.44), channel_id=1, source_target_pairs={{0,4},{4,8},{8,12},{12,0},{1,5},{5,9},{9,13},{13,1},{2,6},{6,10},{... | collective-permute-start | bytes 196616 | tf_op jit(solution)/shard_map/ppermute | solution.py:25
  99.3 1.8 %collective-permute-start.19 = (f32[2,2,32,10,1]{2,1,4,3,0:T(2,128)S(1)}, f32[2,2,32,10,1]{2,1,4,3,0:T(2,128)S(1)}, u32[]{:S(2)}, u32[]{:S(2)}) collective-permute-start(f32[2,2,32,10,1]{2,1,4,3,0:T(2,128)S(1)} %copy.434), channel_id=1, source_target_pairs={{0,2},{2,0},{1,3},{3,1},{4,6},{6,4},{5,7},{7,5},{8,10},{10,8},{9,1... | collective-permute-start | bytes 15368 | tf_op jit(solution)/shard_map/ppermute | solution.py:25
  99.4 1.8 %collective-permute-start.18 = (f32[2,2,32,10,1]{2,1,4,3,0:T(2,128)S(1)}, f32[2,2,32,10,1]{2,1,4,3,0:T(2,128)S(1)}, u32[]{:S(2)}, u32[]{:S(2)}) collective-permute-start(f32[2,2,32,10,1]{2,1,4,3,0:T(2,128)S(1)} %copy.432), channel_id=1, source_target_pairs={{2,0},{0,2},{3,1},{1,3},{6,4},{4,6},{7,5},{5,7},{10,8},{8,10},{11,... | collective-permute-start | bytes 15368 | tf_op jit(solution)/shard_map/ppermute | solution.py:26
  105.4 8.5 %collective-permute-start.20 = (f32[2,2,32,1,128]{2,4,3,0,1:T(8,128)S(1)}, f32[2,2,32,1,128]{2,4,3,0,1:T(8,128)S(1)}, u32[]{:S(2)}, u32[]{:S(2)}) collective-permute-start(f32[2,2,32,1,128]{2,4,3,0,1:T(8,128)S(1)} %get-tuple-element.39), channel_id=1, source_target_pairs={{4,0},{8,4},{12,8},{0,12},{5,1},{9,5},{13,9},{1,13},{6,2},{10,6},{... | collective-permute-start | bytes 196616 | tf_op jit(solution)/shard_map/ppermute | solution.py:26
  107.2 13.0 %collective-permute-start.21 = (f32[2,2,32,1,128]{2,4,3,0,1:T(8,128)S(1)}, f32[2,2,32,1,128]{2,4,3,0,1:T(8,128)S(1)}, u32[]{:S(2)}, u32[]{:S(2)}) collective-permute-start(f32[2,2,32,1,128]{2,4,3,0,1:T(8,128)S(1)} %get-tuple-element.38), channel_id=1, source_target_pairs={{0,4},{4,8},{8,12},{12,0},{1,5},{5,9},{9,13},{13,1},{2,6},{6,10},{... | collective-permute-start | bytes 196616 | tf_op jit(solution)/shard_map/ppermute | solution.py:25
  120.3 1.8 %collective-permute-start.23 = (f32[2,2,32,10,1]{2,1,4,3,0:T(2,128)S(1)}, f32[2,2,32,10,1]{2,1,4,3,0:T(2,128)S(1)}, u32[]{:S(2)}, u32[]{:S(2)}) collective-permute-start(f32[2,2,32,10,1]{2,1,4,3,0:T(2,128)S(1)} %copy.439), channel_id=1, source_target_pairs={{0,2},{2,0},{1,3},{3,1},{4,6},{6,4},{5,7},{7,5},{8,10},{10,8},{9,1... | collective-permute-start | bytes 15368 | tf_op jit(solution)/shard_map/ppermute | solution.py:25
  120.4 1.8 %collective-permute-start.22 = (f32[2,2,32,10,1]{2,1,4,3,0:T(2,128)S(1)}, f32[2,2,32,10,1]{2,1,4,3,0:T(2,128)S(1)}, u32[]{:S(2)}, u32[]{:S(2)}) collective-permute-start(f32[2,2,32,10,1]{2,1,4,3,0:T(2,128)S(1)} %copy.437), channel_id=1, source_target_pairs={{2,0},{0,2},{3,1},{1,3},{6,4},{4,6},{7,5},{5,7},{10,8},{8,10},{11,... | collective-permute-start | bytes 15368 | tf_op jit(solution)/shard_map/ppermute | solution.py:26
  125.1 8.5 %collective-permute-start.24 = (f32[2,2,32,1,128]{2,4,3,0,1:T(8,128)S(1)}, f32[2,2,32,1,128]{2,4,3,0,1:T(8,128)S(1)}, u32[]{:S(2)}, u32[]{:S(2)}) collective-permute-start(f32[2,2,32,1,128]{2,4,3,0,1:T(8,128)S(1)} %get-tuple-element.33), channel_id=1, source_target_pairs={{4,0},{8,4},{12,8},{0,12},{5,1},{9,5},{13,9},{1,13},{6,2},{10,6},{... | collective-permute-start | bytes 196616 | tf_op jit(solution)/shard_map/ppermute | solution.py:26
  126.8 13.4 %collective-permute-start.25 = (f32[2,2,32,1,128]{2,4,3,0,1:T(8,128)S(1)}, f32[2,2,32,1,128]{2,4,3,0,1:T(8,128)S(1)}, u32[]{:S(2)}, u32[]{:S(2)}) collective-permute-start(f32[2,2,32,1,128]{2,4,3,0,1:T(8,128)S(1)} %get-tuple-element.32), channel_id=1, source_target_pairs={{0,4},{4,8},{8,12},{12,0},{1,5},{5,9},{9,13},{13,1},{2,6},{6,10},{... | collective-permute-start | bytes 196616 | tf_op jit(solution)/shard_map/ppermute | solution.py:25
  140.2 1.5 collective-permute-start.27
  140.3 1.4 collective-permute-start.26
  (3 other events, 5.9 us)
Sparse Core Ops, SparseCore 0:
  145.0 9.6 reduce-scatter.1
where the time goes:
time: 162 us
  waiting for transfers between devices  65.2 us (40%)
  other arithmetic  50.6 us (31%)
  starting transfers between devices  23.9 us (15%)
  between operations  14.2 us (9%)
  local copies, waits for them, and re-layouts  7.72 us (5%)
    ppermute x14, waiting for transfers between devices, with_halo(): before = lax.ppermute(last, axis, up)  32.2 us
    ppermute x14, waiting for transfers between devices, with_halo(): after = lax.ppermute(leading, axis, down)  23.2 us
    ppermute x14, starting transfers between devices, with_halo(): after = lax.ppermute(leading, axis, down)  22.1 us
    reduce_scatter x1, waiting for transfers between devices, on_device(): lax.psum_scatter(partial_value, 'dose', scatter_dimension=0, tiled=True)  9.82 us
    sub x5, other arithmetic, diffuse(): return (lateral, upward + downward - 2.0 * center)  9.21 us
    sub x5, other arithmetic, diffuse(): padded[..., 2:, 1:-1] + padded[..., :-2, 1:-1] + padded[..., 1:-1, 2:]  7.74 us
    another operation x3, other arithmetic, on_device(): fields = jnp.stack((acid_now, quench_now), axis=1)  6.37 us
    another operation x9, other arithmetic, retreat(): return (jnp.stack((next_acid, next_quench), axis=1), next_protect)  4.88 us
  transfers between devices with their start and end apart: 29, of which 11 were waited for; matrix products, arithmetic and copies ran while one was open for 24% of the time, Pallas kernels for 0%

commit v1 on v0

v1 whole, which is shorter than its diff:
```python
import functools

import jax
import jax.numpy as jnp
from jax import lax
from jax.experimental import pallas as pl
from jax.experimental.pallas import tpu as pltpu
from jax.sharding import PartitionSpec as P

exposure_rate = 1.0
neutral_rate = 0.8
deprotect_rate = 0.5
acid_lateral = 0.23
acid_depth = 0.02
base_lateral = 0.2
base_depth = 0.02

MESH = pl.DeviceIdType.MESH
IMG, QUE, COT = 5, 4, 3


def kernel(
    sizes, image, quench_in, cot_in, levels, index, out,
    raw, img, que, cot, cot_away, a0, a1, a2, a3, q1, q2,
    b3, b2a, b2q, b1a, b1q, part, got, load_sem, send_sem, recv_sem,
):
    depth, rows, lanes, doses, slab = sizes
    first, last = IMG, IMG + rows
    ring = lax.axis_size("tx")
    tx, ty, dose = lax.axis_index("tx"), lax.axis_index("ty"), lax.axis_index("dose")
    before, after = lax.rem(tx + ring - 1, ring), lax.rem(tx + 1, ring)
    away = 1 - ty
    peers = [lax.rem(dose + k, doses) for k in range(doses)]

    loads = []
    for k, src in enumerate((image, quench_in, cot_in.at[ty], cot_in.at[away])):
        loads.append(pltpu.make_async_copy(src, raw.at[k], load_sem.at[k]))
        loads[-1].start()

    barrier = pltpu.get_barrier_semaphore()
    partners = [{"ty": away}]
    for side in (before, after):
        partners += [{"tx": side}, {"tx": side, "ty": away}]
    for k in range(1, doses):
        partners += [{"dose": peers[k]}]
        partners += [{"dose": lax.rem(dose + k, doses), "ty": away}]
    for device in partners:
        pl.semaphore_signal(barrier, inc=1, device_id=device, device_id_type=MESH)

    counter = [0]

    def send(src, dst, device):
        k = counter[0]
        counter[0] += 1
        copy = pltpu.make_async_remote_copy(
            src_ref=src, dst_ref=dst, send_sem=send_sem.at[k], recv_sem=recv_sem.at[k],
            device_id=device, device_id_type=MESH,
        )
        copy.start()
        return copy

    def turn(k, ref):
        for r in range(rows):
            ref[first + r] = raw[k, pl.ds(r, depth, stride=rows), :]

    def send_rims(src, dst, width, where):
        return [
            send(src.at[pl.ds(first, width)], dst.at[pl.ds(last, width)], dict(tx=before, **where)),
            send(src.at[pl.ds(last - width, width)], dst.at[pl.ds(first - width, width)], dict(tx=after, **where)),
        ]

    def pass_rims(ref, width):
        return [
            send(ref.at[0, pl.ds(last, width)], ref.at[1, pl.ds(last, width)], {"ty": away}),
            send(ref.at[0, pl.ds(first - width, width)], ref.at[1, pl.ds(first - width, width)], {"ty": away}),
        ]

    own = pl.ds(first, rows)
    loads[0].wait()
    turn(0, img.at[0])
    pl.semaphore_wait(barrier, len(partners))
    img_rims = send_rims(img.at[0], img.at[0], IMG, {})
    img_half = send(img.at[0, own], img.at[1, own], {"ty": away})
    loads[1].wait()
    turn(1, que.at[0])
    que_rims = send_rims(que.at[0], que.at[0], QUE, {})
    que_half = send(que.at[0, own], que.at[1, own], {"ty": away})
    loads[2].wait()
    turn(2, cot.at[0])
    loads[3].wait()
    turn(3, cot_away)
    cot_rims = send_rims(cot.at[0], cot.at[0], COT, {})
    cot_rims += send_rims(cot_away, cot.at[1], COT, {"ty": away})
    cot_half = send(cot_away.at[own], cot.at[1, own], {"ty": away})

    dose_value = levels[index[ty]]
    scale = -exposure_rate * dose_value

    lane = lax.broadcasted_iota(jnp.int32, (depth, lanes), 1)
    layer = lax.broadcasted_iota(jnp.int32, (depth, lanes), 0)
    left_edge, right_edge = lane == 0, lane == lanes - 1
    top, bottom = layer == 0, layer == depth - 1

    def spread(ref, j, lateral, vertical):
        here = [ref[0, j], ref[1, j]]
        right = [pltpu.roll(f, 1, 1) for f in here]
        left = [pltpu.roll(f, lanes - 1, 1) for f in here]
        result = []
        for h in range(2):
            f = here[h]
            side = jnp.where(left_edge, right[1 - h], right[h])
            side += jnp.where(right_edge, left[1 - h], left[h])
            side += ref[h, j - 1] + ref[h, j + 1]
            near = jnp.where(top, f, pltpu.roll(f, 1, 0))
            near += jnp.where(bottom, f, pltpu.roll(f, depth - 1, 0))
            moved = (1.0 - 4.0 * lateral - 2.0 * vertical) * f + lateral * side + vertical * near
            result.append((f, moved))
        return result

    def each_row(body, low, high, skip_low=None, skip_high=None):
        if skip_low is None:
            skip_low = skip_high = high
        gap, count = skip_high - skip_low, (high - low) - (skip_high - skip_low)

        def step(i, carry):
            j = i + low
            body(jnp.where(j < skip_low, j, j + gap) if gap else j)
            return carry

        lax.fori_loop(0, count, step, 0)

    def expose(h):
        def body(j):
            a0[h, j] = 1.0 - jnp.exp(scale * img[h, j])
        return body

    def forward(a, q, a_next, q_next):
        def body(j):
            acid = spread(a, j, acid_lateral, acid_depth)
            base = spread(q, j, base_lateral, base_depth) if q_next is not None else None
            for h in range(2):
                now = acid[h][0]
                if base is None:
                    a_next[h, j] = acid[h][1] - neutral_rate * now * q[h, j]
                else:
                    reaction = neutral_rate * now * base[h][0]
                    a_next[h, j] = acid[h][1] - reaction
                    q_next[h, j] = base[h][1] - reaction
        return body

    def rest(a, h, j):
        return 1.0 - deprotect_rate * a[h, j]

    def source(h, j, others):
        value = deprotect_rate * cot[h, j]
        for a in others:
            value = value * rest(a, h, j)
        return value

    def back3(j):
        for h in range(2):
            b3[h, j] = -source(h, j, (a0, a1, a2))

    def back2(j):
        acid = spread(b3, j, acid_lateral, acid_depth)
        for h in range(2):
            s, moved = acid[h]
            pull = neutral_rate * s
            b2a[h, j] = moved - pull * q2[h, j] - source(h, j, (a0, a1, a3))
            b2q[h, j] = -pull * a2[h, j]

    def back1(j):
        acid = spread(b2a, j, acid_lateral, acid_depth)
        base = spread(b2q, j, base_lateral, base_depth)
        for h in range(2):
            pull = neutral_rate * (acid[h][0] + base[h][0])
            b1a[h, j] = acid[h][1] - pull * q1[h, j] - source(h, j, (a0, a2, a3))
            b1q[h, j] = base[h][1] - pull * a1[h, j]

    def back0(j):
        acid = spread(b1a, j, acid_lateral, acid_depth)
        for h in range(2):
            pull = neutral_rate * (acid[h][0] + b1q[h, j])
            value = acid[h][1] - pull * que[h, j] - source(h, j, (a1, a2, a3))
            absorbed = jnp.exp(scale * img[h, j])
            part[h, j - first] = value * (exposure_rate * dose_value) * absorbed

    each_row(expose(0), first, last)
    img_half.wait_recv()
    each_row(expose(1), first, last)
    que_half.wait_recv()
    each_row(forward(a0, que, a1, q1), first + 1, last - 1)
    for copy in img_rims:
        copy.wait_recv()
    img_pass = pass_rims(img, IMG)
    each_row(forward(a1, q1, a2, q2), first + 2, last - 2)
    each_row(forward(a2, q2, a3, None), first + 3, last - 3)
    each_row(expose(0), 0, last + IMG, first, last)
    for copy in que_rims:
        copy.wait_recv()
    que_pass = pass_rims(que, QUE)
    for copy in img_pass:
        copy.wait_recv()
    each_row(expose(1), 0, last + IMG, first, last)
    for copy in que_pass:
        copy.wait_recv()
    each_row(forward(a0, que, a1, q1), first - 4, last + 4, first + 1, last - 1)
    each_row(forward(a1, q1, a2, q2), first - 3, last + 3, first + 2, last - 2)
    each_row(forward(a2, q2, a3, None), first - 2, last + 2, first + 3, last - 3)
    cot_half.wait_recv()
    each_row(back3, first, last)
    for copy in cot_rims:
        copy.wait_recv()
    each_row(back3, first - 3, last + 3, first, last)
    each_row(back2, first - 2, last + 2)
    each_row(back1, first - 1, last + 1)
    each_row(back0, first, last)

    def layers(k):
        return pl.ds(pl.multiple_of(peers[k] * slab, slab), slab)

    sums = []
    for k in range(1, doses):
        for h in (1, 0):
            where = {"dose": peers[k]} if h == 0 else {"dose": peers[k], "ty": away}
            sums.append(send(part.at[h, :, layers(k)], got.at[h, k], where))
    sums.append(send(part.at[1, :, layers(0)], got.at[1, 0], {"ty": away}))
    for copy in sums:
        copy.wait_recv()
    for r in range(rows):
        total = part[0, r, layers(0), :]
        for h in range(2):
            for k in range(doses):
                if h or k:
                    total += got[h, k, r]
        out[pl.ds(r, slab, stride=rows), :] = total
    for copy in img_rims + [img_half] + que_rims + [que_half] + cot_rims + [cot_half] + img_pass + que_pass + sums:
        copy.wait_send()


def on_device(aerial_image, quencher, cotangent, dose_levels, dose_index):
    depth, rows, lanes = aerial_image.shape
    doses = lax.axis_size("dose")
    slab = depth // doses
    assert cotangent.shape[0] == 2 and lax.axis_size("ty") == 2 and rows >= IMG
    wide = rows + 2 * IMG
    flat = (depth * rows, lanes)
    field = pltpu.VMEM((2, wide, depth, lanes), jnp.float32)
    copies = 15 + 2 * doses - 1
    vmem = pl.BlockSpec(memory_space=pltpu.VMEM)
    smem = pl.BlockSpec(memory_space=pltpu.SMEM)
    anywhere = pl.BlockSpec(memory_space=pl.ANY)
    out = pl.pallas_call(
        functools.partial(kernel, (depth, rows, lanes, doses, slab)),
        out_shape=jax.ShapeDtypeStruct((slab * rows, lanes), jnp.float32),
        in_specs=[anywhere, anywhere, anywhere, smem, smem],
        out_specs=vmem,
        scratch_shapes=[
            pltpu.VMEM((4,) + flat, jnp.float32),
            field, field, field,
            pltpu.VMEM((wide, depth, lanes), jnp.float32),
            field, field, field, field, field, field,
            field, field, field, field, field,
            pltpu.VMEM((2, rows, depth, lanes), jnp.float32),
            pltpu.VMEM((2, doses, rows, slab, lanes), jnp.float32),
            pltpu.SemaphoreType.DMA((4,)),
            pltpu.SemaphoreType.DMA((copies,)),
            pltpu.SemaphoreType.DMA((copies,)),
        ],
        compiler_params=pltpu.CompilerParams(
            collective_id=0, has_side_effects=True, vmem_limit_bytes=24 * 1024 * 1024
        ),
        name="bake_adjoint",
    )(
        aerial_image.reshape(flat),
        quencher.reshape(flat),
        cotangent.reshape((2,) + flat),
        dose_levels,
        dose_index,
    )
    return out.reshape(slab, rows, lanes)


def solution(mesh):
    placed = (
        P("focus", "tx", "ty"),
        P(None, "tx", "ty"),
        P(("focus", "dose"), None, "tx", "ty"),
        P(),
        P(("focus", "dose")),
    )
    return jax.shard_map(
        on_device,
        mesh=mesh,
        in_specs=placed,
        out_specs=P(("focus", "dose"), "tx", "ty"),
        check_vma=False,
    )
```

time: 162 us -> 31.1 us (0.19)
  waiting for transfers between devices: 65.2 us -> 0 us
  other arithmetic: 50.6 us -> 0 us
  Pallas kernels: 0 us -> 26.9 us
  starting transfers between devices: 23.9 us -> 0 us
  between operations: 14.2 us -> 0.01 us
  local copies, waits for them, and re-layouts: 7.72 us -> 4.06 us
    ppermute x28 -> x0, waiting for transfers between devices: 55.4 us -> none  [the longest x14 32.2 us: with_halo(): before = lax.ppermute(last, axis, up)]
    pallas_call x0 -> x1, Pallas kernels: none -> 26.9 us  [on_device(): pl.pallas_call(functools.partial(kernel, (depth, rows, lanes, doses, slab...]
    sub x18 -> x0, other arithmetic: 24.5 us -> none  [the longest x5 9.21 us: diffuse(): return (lateral, upward + downward - 2.0 * center)]
    ppermute x28 -> x0, starting transfers between devices: 23.9 us -> none  [the longest x14 22.1 us: with_halo(): after = lax.ppermute(leading, axis, down)]
    another operation x18 -> x0, other arithmetic: 14.5 us -> none  [the longest x3 6.37 us: on_device(): fields = jnp.stack((acid_now, quench_now), axis=1)]
    reduce_scatter x1 -> x0, waiting for transfers between devices: 9.82 us -> none  [on_device(): lax.psum_scatter(partial_value, 'dose', scatter_dimension=0, tiled=True)]
    add x1 -> x0, other arithmetic: 4.46 us -> none  [diffuse(): padded[..., 2:, 1:-1] + padded[..., :-2, 1:-1] + padded[..., 1:-1, 2:]]
    reduce_sum x2 -> x0, other arithmetic: 3.23 us -> none  [the longest x1 2.3 us: on_device(): jnp.sum(adjoint[:, 0] * exposure_rate * dose_col * absorbed, axis=0)]
  transfers between devices with their start and end apart: 29 -> 0, of which waited for: 11 -> 0; matrix products, arithmetic and copies ran while one was open for 24% -> 0% of each run, Pallas kernels for 0% -> 0%
where the time goes in v1:
time: 31.1 us; the launch traced here: 31 us
  Pallas kernels  26.9 us (86%)
  local copies, waits for them, and re-layouts  4.06 us (13%)
    pallas_call x1, Pallas kernels, on_device(): pl.pallas_call(functools.partial(kernel, (depth, rows, lanes, doses, slab...  26.9 us
    unnamed x11, local copies, waits for them, and re-layouts  4.06 us

profile of v1, /device:TPU:0, one launch (start us, length us, event | category | flops | bytes accessed | tf_op | source)
XLA Modules:
  0.0 31.0 jit_solution(2793618321083918227)
XLA Ops:
  0.0 0.0 copy-start.3
  0.0 0.0 copy-start.4
  0.0 0.7 %copy-done.3 = f32[16]{0:T(128)S(1)} copy-done((f32[16]{0:T(128)S(1)}, f32[16]{0:T(128)}, u32[]{:S(2)}) %copy-start.3) | copy-done | bytes 88
  0.7 0.0 copy-done.4
  0.7 0.0 copy-start
  0.7 0.9 %copy-done = f32[2,32,8,128]{3,2,1,0:T(8,128)S(1)} copy-done((f32[2,32,8,128]{3,2,1,0:T(8,128)S(1)}, f32[2,32,8,128]{3,2,1,0:T(8,128)}, u32[]{:S(2)}) %copy-start) | copy-done | bytes 262168
  1.6 0.0 copy-start.1
  1.6 0.9 %copy-done.1 = f32[32,8,128]{2,1,0:T(8,128)S(1)} copy-done((f32[32,8,128]{2,1,0:T(8,128)S(1)}, f32[32,8,128]{2,1,0:T(8,128)}, u32[]{:S(2)}) %copy-start.1) | copy-done | bytes 131096
  2.5 0.0 copy-start.2
  2.5 0.9 %copy-done.2 = f32[32,8,128]{2,1,0:T(8,128)S(1)} copy-done((f32[32,8,128]{2,1,0:T(8,128)S(1)}, f32[32,8,128]{2,1,0:T(8,128)}, u32[]{:S(2)}) %copy-start.2) | copy-done | bytes 131096
  3.4 26.9 %bake_adjoint.1 = f32[128,128]{1,0:T(8,128)S(1)} custom-call(f32[256,128]{1,0:T(8,128)S(1)} %bitcast.6, f32[256,128]{1,0:T(8,128)S(1)} %bitcast.7, f32[2,256,128]{2,1,0:T(8,128)S(1)} %bitcast.5, f32[16]{0:T(128)S(1)} %copy-done.3, s32[2]{0:T(128)S(1)} %copy-done.4), custom_call_target="tpu_custom_call" | custom-call | tf_op jit(solution)/shard_map/bake_adjoint/pallas_call | solution.py:253
  30.3 0.6 %copy.7 = f32[16,8,128]{2,1,0:T(8,128)} copy(f32[16,8,128]{2,1,0:T(8,128)S(1)} %bitcast.4) | data formatting | bytes 131072
Async XLA Ops:
  0.0 0.7 %copy-start.3 = (f32[16]{0:T(128)S(1)}, f32[16]{0:T(128)}, u32[]{:S(2)}) copy-start(f32[16]{0:T(128)} %levels.1) | copy-start | bytes 196
  0.0 0.7 %copy-start.4 = (s32[2]{0:T(128)S(1)}, s32[2]{0:T(128)}, u32[]{:S(2)}) copy-start(s32[2]{0:T(128)} %index.1) | copy-start | bytes 28
  0.7 0.9 %copy-start = (f32[2,32,8,128]{3,2,1,0:T(8,128)S(1)}, f32[2,32,8,128]{3,2,1,0:T(8,128)}, u32[]{:S(2)}) copy-start(f32[2,32,8,128]{3,2,1,0:T(8,128)} %param.7) | copy-start | bytes 786436
  1.6 0.9 %copy-start.1 = (f32[32,8,128]{2,1,0:T(8,128)S(1)}, f32[32,8,128]{2,1,0:T(8,128)}, u32[]{:S(2)}) copy-start(f32[32,8,128]{2,1,0:T(8,128)} %param.5) | copy-start | bytes 393220
  2.5 0.9 %copy-start.2 = (f32[32,8,128]{2,1,0:T(8,128)S(1)}, f32[32,8,128]{2,1,0:T(8,128)}, u32[]{:S(2)}) copy-start(f32[32,8,128]{2,1,0:T(8,128)} %param.6) | copy-start | bytes 393220

commit v2 on v1

v2 whole, which is shorter than its diff:
```python
import functools

import jax
import jax.numpy as jnp
from jax import lax
from jax.experimental import pallas as pl
from jax.experimental.pallas import tpu as pltpu
from jax.sharding import PartitionSpec as P

exposure_rate = 1.0
neutral_rate = 0.8
deprotect_rate = 0.5
acid_lateral = 0.23
acid_depth = 0.02
base_lateral = 0.2
base_depth = 0.02

MESH = pl.DeviceIdType.MESH
IMG, QUE, COT = 5, 4, 3


def kernel(
    sizes, image, quench_in, cot_in, levels_in, index_in, out,
    raw, img, que, cot, cot_away, a0, a1, a2, a3, q1, q2, kept01,
    b3, b2a, b2q, b1a, b1q, weight, part, half_sum, got, levels, index,
    load_sem, send_sem, recv_sem,
):
    depth, rows, lanes, doses, slab = sizes
    tiles = depth // 8
    first, last = IMG, IMG + rows
    ring = lax.axis_size("tx")
    tx, ty, dose = lax.axis_index("tx"), lax.axis_index("ty"), lax.axis_index("dose")
    before, after = lax.rem(tx + ring - 1, ring), lax.rem(tx + 1, ring)
    away = 1 - ty
    peers = [lax.rem(dose + k, doses) for k in range(doses)]

    loads = []
    for k, src in enumerate((image, quench_in, cot_in.at[ty], cot_in.at[away])):
        loads.append(pltpu.make_async_copy(src, raw.at[k], load_sem.at[k]))
        loads[-1].start()
    for k, (src, dst) in enumerate(((levels_in, levels), (index_in, index))):
        loads.append(pltpu.make_async_copy(src, dst, load_sem.at[4 + k]))
        loads[-1].start()

    barrier = pltpu.get_barrier_semaphore()
    partners = [{"ty": away}]
    for side in (before, after):
        partners += [{"tx": side}, {"tx": side, "ty": away}]
    for k in range(1, doses):
        partners += [{"dose": peers[k]}]
    for device in partners:
        pl.semaphore_signal(barrier, inc=1, device_id=device, device_id_type=MESH)

    counter = [0]

    def send(src, dst, device):
        k = counter[0]
        counter[0] += 1
        copy = pltpu.make_async_remote_copy(
            src_ref=src, dst_ref=dst, send_sem=send_sem.at[k], recv_sem=recv_sem.at[k],
            device_id=device, device_id_type=MESH,
        )
        copy.start()
        return copy

    def turn(k, ref):
        for r in range(rows):
            for t in range(tiles):
                ref[first + r, t] = raw[k, pl.ds(t * rows + r, 8, stride=tiles * rows), :]

    def send_rims(src, dst, width, where):
        return [
            send(src.at[pl.ds(last - width, width)], dst.at[pl.ds(first - width, width)], dict(tx=after, **where)),
            send(src.at[pl.ds(first, width)], dst.at[pl.ds(last, width)], dict(tx=before, **where)),
        ]

    def pass_rims(ref, width):
        return [
            send(ref.at[0, pl.ds(first - width, width)], ref.at[1, pl.ds(first - width, width)], {"ty": away}),
            send(ref.at[0, pl.ds(last, width)], ref.at[1, pl.ds(last, width)], {"ty": away}),
        ]

    own = pl.ds(first, rows)
    loads[0].wait()
    turn(0, img.at[0])
    pl.semaphore_wait(barrier, len(partners))
    img_rims = send_rims(img.at[0], img.at[0], IMG, {})
    img_half = send(img.at[0, own], img.at[1, own], {"ty": away})
    loads[1].wait()
    turn(1, que.at[0])
    que_rims = send_rims(que.at[0], que.at[0], QUE, {})
    que_half = send(que.at[0, own], que.at[1, own], {"ty": away})
    loads[2].wait()
    turn(2, cot.at[0])
    loads[3].wait()
    turn(3, cot_away)
    cot_near = send_rims(cot.at[0], cot.at[0], COT, {})
    cot_far = send_rims(cot_away, cot.at[1], COT, {"ty": away})
    cot_half = send(cot_away.at[own], cot.at[1, own], {"ty": away})

    loads[4].wait()
    loads[5].wait()
    dose_value = levels[index[ty]]
    scale = -exposure_rate * dose_value

    lane = lax.broadcasted_iota(jnp.int32, (tiles, 8, lanes), 2)
    layer = lax.broadcasted_iota(jnp.int32, (8, lanes), 0)
    left_edge, right_edge = lane == 0, lane == lanes - 1
    top, bottom = layer == 0, layer == 7

    def spread(ref, j, lateral, vertical):
        here = [ref[0, j], ref[1, j]]
        right = [pltpu.roll(f, 1, 2) for f in here]
        left = [pltpu.roll(f, lanes - 1, 2) for f in here]
        result = []
        for h in range(2):
            f = here[h]
            side = jnp.where(left_edge, right[1 - h], right[h])
            side += jnp.where(right_edge, left[1 - h], left[h])
            side += ref[h, j - 1] + ref[h, j + 1]
            above = jnp.where(top, f[0], pltpu.roll(f[tiles - 1], 1, 0))
            below = jnp.where(bottom, f[tiles - 1], pltpu.roll(f[0], 7, 0))
            near = jnp.concatenate((above[None], f[:-1]), 0) + jnp.concatenate((f[1:], below[None]), 0)
            moved = (1.0 - 4.0 * lateral - 2.0 * vertical) * f + lateral * side + vertical * near
            result.append((f, moved))
        return result

    def each_row(body, low, high, skip_low=None, skip_high=None):
        if skip_low is None:
            skip_low = skip_high = high
        gap, count = skip_high - skip_low, (high - low) - (skip_high - skip_low)

        def step(i, carry):
            j = i + low
            body(jnp.where(j < skip_low, j, j + gap) if gap else j)
            return carry

        lax.fori_loop(0, count, step, 0)

    def expose(h):
        def body(j):
            a0[h, j] = 1.0 - jnp.exp(scale * img[h, j])
        return body

    def rest(acid):
        return 1.0 - deprotect_rate * acid

    def forward0(j):
        acid = spread(a0, j, acid_lateral, acid_depth)
        base = spread(que, j, base_lateral, base_depth)
        for h in range(2):
            reaction = neutral_rate * acid[h][0] * base[h][0]
            a1[h, j] = acid[h][1] - reaction
            q1[h, j] = base[h][1] - reaction

    def forward1(j):
        acid = spread(a1, j, acid_lateral, acid_depth)
        base = spread(q1, j, base_lateral, base_depth)
        for h in range(2):
            reaction = neutral_rate * acid[h][0] * base[h][0]
            a2[h, j] = acid[h][1] - reaction
            q2[h, j] = base[h][1] - reaction
            kept01[h, j] = rest(a0[h, j]) * rest(acid[h][0])

    def forward2(j):
        acid = spread(a2, j, acid_lateral, acid_depth)
        for h in range(2):
            a3[h, j] = acid[h][1] - neutral_rate * acid[h][0] * q2[h, j]

    def back3(j):
        for h in range(2):
            b3[h, j] = -deprotect_rate * cot[h, j] * kept01[h, j] * rest(a2[h, j])

    def back2(j):
        acid = spread(b3, j, acid_lateral, acid_depth)
        for h in range(2):
            s, moved = acid[h]
            pull = neutral_rate * s
            acid_old = a2[h, j]
            arrived = deprotect_rate * cot[h, j] * rest(a3[h, j])
            b2a[h, j] = moved - pull * q2[h, j] - kept01[h, j] * arrived
            b2q[h, j] = -pull * acid_old
            weight[h, j] = arrived * rest(acid_old)

    def back1(j):
        acid = spread(b2a, j, acid_lateral, acid_depth)
        base = spread(b2q, j, base_lateral, base_depth)
        for h in range(2):
            pull = neutral_rate * (acid[h][0] + base[h][0])
            b1a[h, j] = acid[h][1] - pull * q1[h, j] - rest(a0[h, j]) * weight[h, j]
            b1q[h, j] = base[h][1] - pull * a1[h, j]

    def back0(j):
        acid = spread(b1a, j, acid_lateral, acid_depth)
        for h in range(2):
            pull = neutral_rate * (acid[h][0] + b1q[h, j])
            value = acid[h][1] - pull * que[h, j] - rest(a1[h, j]) * weight[h, j]
            value = value * (exposure_rate * dose_value) * jnp.exp(scale * img[h, j])
            for t in range(tiles):
                part[h, j - first, pl.ds(t, 8, stride=tiles), :] = value[t]

    each_row(expose(0), first, last)
    img_half.wait_recv()
    each_row(expose(1), first, last)
    que_half.wait_recv()
    each_row(forward0, first + 1, last - 1)
    for copy in img_rims:
        copy.wait_recv()
    img_pass = pass_rims(img, IMG)
    each_row(forward1, first + 2, last - 2)
    each_row(forward2, first + 3, last - 3)
    each_row(expose(0), 0, last + IMG, first, last)
    for copy in que_rims:
        copy.wait_recv()
    que_pass = pass_rims(que, QUE)
    for copy in img_pass:
        copy.wait_recv()
    each_row(expose(1), 0, last + IMG, first, last)
    for copy in que_pass:
        copy.wait_recv()
    each_row(forward0, first - 4, last + 4, first + 1, last - 1)
    each_row(forward1, first - 3, last + 3, first + 2, last - 2)
    each_row(forward2, first - 2, last + 2, first + 3, last - 3)
    cot_half.wait_recv()
    each_row(back3, first, last)
    each_row(back2, first + 1, last - 1)
    each_row(back1, first + 2, last - 2)
    each_row(back0, first + 3, last - 3)

    middle = rows // 2
    chunks = (pl.ds(0, middle), pl.ds(middle, rows - middle))
    halves = []
    for side, bounds in enumerate(
        (
            ((first - 3, first), (first - 2, first + 1), (first - 1, first + 2), (first, first + 3)),
            ((last, last + 3), (last - 1, last + 2), (last - 2, last + 1), (last - 3, last)),
        )
    ):
        cot_near[side].wait_recv()
        cot_far[side].wait_recv()
        for body, (low, high) in zip((back3, back2, back1, back0), bounds):
            each_row(body, low, high)
        halves.append(send(part.at[1, chunks[side]], half_sum.at[chunks[side]], {"ty": away}))

    def layers(k):
        return pl.ds(pl.multiple_of(peers[k] * slab, slab), slab)

    sums = []
    for side in range(2):
        halves[side].wait_recv()
        half_sum[chunks[side]] += part[0, chunks[side]]
        for k in range(1, doses):
            sums.append(send(half_sum.at[chunks[side], layers(k)], got.at[k, chunks[side]], {"dose": peers[k]}))
    for copy in sums:
        copy.wait_recv()
    for r in range(rows):
        total = half_sum[r, layers(0), :]
        for k in range(1, doses):
            total += got[k, r]
        out[pl.ds(r, slab, stride=rows), :] = total
    for copy in (
        img_rims + [img_half] + que_rims + [que_half] + cot_near + cot_far + [cot_half]
        + img_pass + que_pass + halves + sums
    ):
        copy.wait_send()


def on_device(aerial_image, quencher, cotangent, dose_levels, dose_index):
    depth, rows, lanes = aerial_image.shape
    doses = lax.axis_size("dose")
    slab = depth // doses
    assert cotangent.shape[0] == 2 and lax.axis_size("ty") == 2 and rows >= IMG
    wide = rows + 2 * IMG
    flat = (depth * rows, lanes)
    turned = (wide, depth // 8, 8, lanes)
    field = pltpu.VMEM((2,) + turned, jnp.float32)
    copies = 15 + 2 + 2 * (doses - 1)
    vmem = pl.BlockSpec(memory_space=pltpu.VMEM)
    anywhere = pl.BlockSpec(memory_space=pl.ANY)
    out = pl.pallas_call(
        functools.partial(kernel, (depth, rows, lanes, doses, slab)),
        out_shape=jax.ShapeDtypeStruct((slab * rows, lanes), jnp.float32),
        in_specs=[anywhere] * 5,
        out_specs=vmem,
        scratch_shapes=[
            pltpu.VMEM((4,) + flat, jnp.float32),
            field, field, field,
            pltpu.VMEM(turned, jnp.float32),
            field, field, field, field, field, field, field,
            field, field, field, field, field, field,
            pltpu.VMEM((2, rows, depth, lanes), jnp.float32),
            pltpu.VMEM((rows, depth, lanes), jnp.float32),
            pltpu.VMEM((doses, rows, slab, lanes), jnp.float32),
            pltpu.SMEM(dose_levels.shape, jnp.float32),
            pltpu.SMEM(dose_index.shape, jnp.int32),
            pltpu.SemaphoreType.DMA((6,)),
            pltpu.SemaphoreType.DMA((copies,)),
            pltpu.SemaphoreType.DMA((copies,)),
        ],
        compiler_params=pltpu.CompilerParams(
            collective_id=0, has_side_effects=True, vmem_limit_bytes=64 * 1024 * 1024
        ),
        name="bake_adjoint",
    )(
        aerial_image.reshape(flat),
        quencher.reshape(flat),
        cotangent.reshape((2,) + flat),
        dose_levels,
        dose_index,
    )
    return out.reshape(slab, rows, lanes)


def solution(mesh):
    placed = (
        P("focus", "tx", "ty"),
        P(None, "tx", "ty"),
        P(("focus", "dose"), None, "tx", "ty"),
        P(),
        P(("focus", "dose")),
    )
    return jax.shard_map(
        on_device,
        mesh=mesh,
        in_specs=placed,
        out_specs=P(("focus", "dose"), "tx", "ty"),
        check_vma=False,
    )
```

time: 31.1 us -> 27 us (0.87)
  local copies, waits for them, and re-layouts: 4.06 us -> 1.47 us
  Pallas kernels: 26.9 us -> 25.3 us
    unnamed x11 -> x1, local copies, waits for them, and re-layouts: 4.06 us -> 1.47 us
    pallas_call x1, Pallas kernels: 26.9 us -> 25.3 us  [on_device(): pl.pallas_call(functools.partial(kernel, (depth, rows, lanes, doses, slab...]
where the time goes in v2:
time: 27 us; the launch traced here: 26.8 us
  Pallas kernels  25.3 us (94%)
  local copies, waits for them, and re-layouts  1.47 us (5%)
    pallas_call x1, Pallas kernels, on_device(): pl.pallas_call(functools.partial(kernel, (depth, rows, lanes, doses, slab...  25.3 us
    unnamed x1, local copies, waits for them, and re-layouts  1.47 us

profile of v2, /device:TPU:0, one launch (start us, length us, event | category | flops | bytes accessed | tf_op | source)
XLA Modules:
  0.0 26.8 jit_solution(13685041683203970972)
XLA Ops:
  0.0 25.3 %bake_adjoint.1 = f32[128,128]{1,0:T(8,128)} custom-call(f32[256,128]{1,0:T(8,128)} %bitcast.6, f32[256,128]{1,0:T(8,128)} %bitcast.7, f32[2,256,128]{2,1,0:T(8,128)} %bitcast.5, f32[16]{0:T(128)} %levels_in.1, s32[2]{0:T(128)} %index_in.1), custom_call_target="tpu_custom_call" | custom-call | tf_op jit(solution)/shard_map/bake_adjoint/pallas_call | solution.py:280
  25.3 1.5 %copy.7 = f32[16,8,128]{2,1,0:T(8,128)} copy(f32[16,8,128]{2,1,0:T(8,128)} %bitcast.4) | data formatting | bytes 131072

commit v3 on v2

--- a/solution.py
+++ b/solution.py
@@ -16,13 +16,13 @@
 base_depth = 0.02
 
 MESH = pl.DeviceIdType.MESH
-IMG, QUE, COT = 5, 4, 3
+IMG, QUE = 3, 2
 
 
 def kernel(
     sizes, image, quench_in, cot_in, levels_in, index_in, out,
     raw, img, que, cot, cot_away, a0, a1, a2, a3, q1, q2, kept01,
-    b3, b2a, b2q, b1a, b1q, weight, part, half_sum, got, levels, index,
+    b3, b2a, b2q, b1a, b1q, weight, part, half_sum, got, got_low, got_high, levels, index,
     load_sem, send_sem, recv_sem,
 ):
     depth, rows, lanes, doses, slab = sizes
@@ -45,9 +45,8 @@
     barrier = pltpu.get_barrier_semaphore()
     partners = [{"ty": away}]
     for side in (before, after):
-        partners += [{"tx": side}, {"tx": side, "ty": away}]
-    for k in range(1, doses):
-        partners += [{"dose": peers[k]}]
+        partners += [{"tx": side, "dose": peers[k]} for k in range(doses)]
+    partners += [{"dose": peers[k]} for k in range(1, doses)]
     for device in partners:
         pl.semaphore_signal(barrier, inc=1, device_id=device, device_id_type=MESH)
 
@@ -68,10 +67,10 @@
             for t in range(tiles):
                 ref[first + r, t] = raw[k, pl.ds(t * rows + r, 8, stride=tiles * rows), :]
 
-    def send_rims(src, dst, width, where):
+    def send_rims(ref, width):
         return [
-            send(src.at[pl.ds(last - width, width)], dst.at[pl.ds(first - width, width)], dict(tx=after, **where)),
-            send(src.at[pl.ds(first, width)], dst.at[pl.ds(last, width)], dict(tx=before, **where)),
+            send(ref.at[0, pl.ds(last - width, width)], ref.at[0, pl.ds(first - width, width)], {"tx": after}),
+            send(ref.at[0, pl.ds(first, width)], ref.at[0, pl.ds(last, width)], {"tx": before}),
         ]
 
     def pass_rims(ref, width):
@@ -80,23 +79,31 @@
             send(ref.at[0, pl.ds(last, width)], ref.at[1, pl.ds(last, width)], {"ty": away}),
         ]
 
+    def clear(ref, *places):
+        for j in places:
+            for h in range(2):
+                ref[h, j] = jnp.zeros(ref.shape[2:], jnp.float32)
+
     own = pl.ds(first, rows)
     loads[0].wait()
     turn(0, img.at[0])
-    pl.semaphore_wait(barrier, len(partners))
-    img_rims = send_rims(img.at[0], img.at[0], IMG, {})
-    img_half = send(img.at[0, own], img.at[1, own], {"ty": away})
     loads[1].wait()
     turn(1, que.at[0])
-    que_rims = send_rims(que.at[0], que.at[0], QUE, {})
+    pl.semaphore_wait(barrier, len(partners))
+    img_rims = send_rims(img, IMG)
+    que_rims = send_rims(que, QUE)
+    img_half = send(img.at[0, own], img.at[1, own], {"ty": away})
     que_half = send(que.at[0, own], que.at[1, own], {"ty": away})
     loads[2].wait()
     turn(2, cot.at[0])
     loads[3].wait()
     turn(3, cot_away)
-    cot_near = send_rims(cot.at[0], cot.at[0], COT, {})
-    cot_far = send_rims(cot_away, cot.at[1], COT, {"ty": away})
     cot_half = send(cot_away.at[own], cot.at[1, own], {"ty": away})
+    clear(b3, first - 1, last)
+    clear(b2a, first - 2, last + 1)
+    clear(b2q, first - 2, first - 1, last, last + 1)
+    clear(b1a, first - 3, last + 2)
+    clear(b1q, first - 2, last + 1)
 
     loads[4].wait()
     loads[5].wait()
@@ -153,6 +160,11 @@
             a1[h, j] = acid[h][1] - reaction
             q1[h, j] = base[h][1] - reaction
 
+    def forward0_acid(j):
+        acid = spread(a0, j, acid_lateral, acid_depth)
+        for h in range(2):
+            a1[h, j] = acid[h][1] - neutral_rate * acid[h][0] * que[h, j]
+
     def forward1(j):
         acid = spread(a1, j, acid_lateral, acid_depth)
         base = spread(q1, j, base_lateral, base_depth)
@@ -161,6 +173,11 @@
             a2[h, j] = acid[h][1] - reaction
             q2[h, j] = base[h][1] - reaction
             kept01[h, j] = rest(a0[h, j]) * rest(acid[h][0])
+
+    def forward1_acid(j):
+        acid = spread(a1, j, acid_lateral, acid_depth)
+        for h in range(2):
+            a2[h, j] = acid[h][1] - neutral_rate * acid[h][0] * q1[h, j]
 
     def forward2(j):
         acid = spread(a2, j, acid_lateral, acid_depth)
@@ -182,22 +199,26 @@
             b2q[h, j] = -pull * acid_old
             weight[h, j] = arrived * rest(acid_old)
 
-    def back1(j):
+    def back1(j, own_row=True):
         acid = spread(b2a, j, acid_lateral, acid_depth)
         base = spread(b2q, j, base_lateral, base_depth)
         for h in range(2):
             pull = neutral_rate * (acid[h][0] + base[h][0])
-            b1a[h, j] = acid[h][1] - pull * q1[h, j] - rest(a0[h, j]) * weight[h, j]
+            value = acid[h][1] - pull * q1[h, j]
+            b1a[h, j] = value - rest(a0[h, j]) * weight[h, j] if own_row else value
             b1q[h, j] = base[h][1] - pull * a1[h, j]
 
-    def back0(j):
+    def finish(h, j, value):
+        value = value * (exposure_rate * dose_value) * jnp.exp(scale * img[h, j])
+        for t in range(tiles):
+            part[h, j, pl.ds(t, 8, stride=tiles), :] = value[t]
+
+    def back0(j, own_row=True):
         acid = spread(b1a, j, acid_lateral, acid_depth)
         for h in range(2):
             pull = neutral_rate * (acid[h][0] + b1q[h, j])
-            value = acid[h][1] - pull * que[h, j] - rest(a1[h, j]) * weight[h, j]
-            value = value * (exposure_rate * dose_value) * jnp.exp(scale * img[h, j])
-            for t in range(tiles):
-                part[h, j - first, pl.ds(t, 8, stride=tiles), :] = value[t]
+            value = acid[h][1] - pull * que[h, j]
+            finish(h, j, value - rest(a1[h, j]) * weight[h, j] if own_row else value)
 
     each_row(expose(0), first, last)
     img_half.wait_recv()
@@ -207,39 +228,47 @@
     for copy in img_rims:
         copy.wait_recv()
     img_pass = pass_rims(img, IMG)
+    for copy in que_rims:
+        copy.wait_recv()
+    que_pass = pass_rims(que, QUE)
     each_row(forward1, first + 2, last - 2)
     each_row(forward2, first + 3, last - 3)
-    each_row(expose(0), 0, last + IMG, first, last)
-    for copy in que_rims:
-        copy.wait_recv()
-    que_pass = pass_rims(que, QUE)
+    each_row(expose(0), first - 3, last + 3, first, last)
     for copy in img_pass:
         copy.wait_recv()
-    each_row(expose(1), 0, last + IMG, first, last)
+    each_row(expose(1), first - 3, last + 3, first, last)
     for copy in que_pass:
         copy.wait_recv()
-    each_row(forward0, first - 4, last + 4, first + 1, last - 1)
-    each_row(forward1, first - 3, last + 3, first + 2, last - 2)
-    each_row(forward2, first - 2, last + 2, first + 3, last - 3)
+    each_row(forward0_acid, first - 2, last + 2, first - 1, last + 1)
+    each_row(forward0, first - 1, last + 1, first + 1, last - 1)
+    each_row(forward1_acid, first - 1, last + 1, first, last)
+    each_row(forward1, first, last, first + 2, last - 2)
+    each_row(forward2, first, last, first + 3, last - 3)
     cot_half.wait_recv()
     each_row(back3, first, last)
-    each_row(back2, first + 1, last - 1)
-    each_row(back1, first + 2, last - 2)
-    each_row(back0, first + 3, last - 3)
+    each_row(back2, first, last)
+    for h in range(2):
+        for j, inner in ((first - 1, first), (last, last - 1)):
+            b2a[h, j] = acid_lateral * b3[h, inner]
+    each_row(back1, first, last)
+    each_row(functools.partial(back1, own_row=False), first - 1, last + 1, first, last)
+    for h in range(2):
+        for j, inner in ((first - 2, first - 1), (last + 1, last)):
+            b1a[h, j] = acid_lateral * b2a[h, inner]
 
     middle = rows // 2
-    chunks = (pl.ds(0, middle), pl.ds(middle, rows - middle))
+    chunks = (pl.ds(0, first + middle), pl.ds(first + middle, last + IMG - first - middle))
     halves = []
-    for side, bounds in enumerate(
+    for side, (edge, inner, outside, inside) in enumerate(
         (
-            ((first - 3, first), (first - 2, first + 1), (first - 1, first + 2), (first, first + 3)),
-            ((last, last + 3), (last - 1, last + 2), (last - 2, last + 1), (last - 3, last)),
+            (first - 3, first - 2, (first - 2, first), (first, first + middle)),
+            (last + 2, last + 1, (last, last + 2), (first + middle, last)),
         )
     ):
-        cot_near[side].wait_recv()
-        cot_far[side].wait_recv()
-        for body, (low, high) in zip((back3, back2, back1, back0), bounds):
-            each_row(body, low, high)
+        for h in range(2):
+            finish(h, edge, acid_lateral * b1a[h, inner])
+        each_row(functools.partial(back0, own_row=False), *outside)
+        each_row(back0, *inside)
         halves.append(send(part.at[1, chunks[side]], half_sum.at[chunks[side]], {"ty": away}))
 
     def layers(k):
@@ -249,18 +278,34 @@
     for side in range(2):
         halves[side].wait_recv()
         half_sum[chunks[side]] += part[0, chunks[side]]
+        reach, beside, there = (
+            (pl.ds(first - IMG, IMG), before, got_high) if side == 0 else (pl.ds(last, IMG), after, got_low)
+        )
+        for k in range(doses):
+            sums.append(send(half_sum.at[reach, layers(k)], there.at[k], {"tx": beside, "dose": peers[k]}))
+        start, count = (0, middle) if side == 0 else (middle, rows - middle)
         for k in range(1, doses):
-            sums.append(send(half_sum.at[chunks[side], layers(k)], got.at[k, chunks[side]], {"dose": peers[k]}))
+            sums.append(
+                send(
+                    half_sum.at[pl.ds(first + start, count), layers(k)],
+                    got.at[k, pl.ds(start, count)],
+                    {"dose": peers[k]},
+                )
+            )
     for copy in sums:
         copy.wait_recv()
     for r in range(rows):
-        total = half_sum[r, layers(0), :]
+        total = half_sum[first + r, layers(0), :]
         for k in range(1, doses):
             total += got[k, r]
+        for k in range(doses):
+            if r < IMG:
+                total += got_low[k, r]
+            if r >= rows - IMG:
+                total += got_high[k, r - (rows - IMG)]
         out[pl.ds(r, slab, stride=rows), :] = total
     for copy in (
-        img_rims + [img_half] + que_rims + [que_half] + cot_near + cot_far + [cot_half]
-        + img_pass + que_pass + halves + sums
+        img_rims + [img_half] + que_rims + [que_half, cot_half] + img_pass + que_pass + halves + sums
     ):
         copy.wait_send()
 
@@ -269,12 +314,12 @@
     depth, rows, lanes = aerial_image.shape
     doses = lax.axis_size("dose")
     slab = depth // doses
-    assert cotangent.shape[0] == 2 and lax.axis_size("ty") == 2 and rows >= IMG
+    assert cotangent.shape[0] == 2 and lax.axis_size("ty") == 2 and rows >= 2 * IMG
     wide = rows + 2 * IMG
     flat = (depth * rows, lanes)
     turned = (wide, depth // 8, 8, lanes)
     field = pltpu.VMEM((2,) + turned, jnp.float32)
-    copies = 15 + 2 + 2 * (doses - 1)
+    copies = 11 + 2 + 2 * (doses - 1) + 2 * doses
     vmem = pl.BlockSpec(memory_space=pltpu.VMEM)
     anywhere = pl.BlockSpec(memory_space=pl.ANY)
     out = pl.pallas_call(
@@ -288,9 +333,11 @@
             pltpu.VMEM(turned, jnp.float32),
             field, field, field, field, field, field, field,
             field, field, field, field, field, field,
-            pltpu.VMEM((2, rows, depth, lanes), jnp.float32),
-            pltpu.VMEM((rows, depth, lanes), jnp.float32),
+            pltpu.VMEM((2, wide, depth, lanes), jnp.float32),
+            pltpu.VMEM((wide, depth, lanes), jnp.float32),
             pltpu.VMEM((doses, rows, slab, lanes), jnp.float32),
+            pltpu.VMEM((doses, IMG, slab, lanes), jnp.float32),
+            pltpu.VMEM((doses, IMG, slab, lanes), jnp.float32),
             pltpu.SMEM(dose_levels.shape, jnp.float32),
             pltpu.SMEM(dose_index.shape, jnp.int32),
             pltpu.SemaphoreType.DMA((6,)),

time: 27 us -> 25.8 us (0.956)
  Pallas kernels: 25.3 us -> 24.2 us
    pallas_call x1, Pallas kernels: 25.3 us -> 24.2 us  [on_device(): pl.pallas_call(functools.partial(kernel, (depth, rows, lanes, doses, slab...]
where the time goes in v3:
time: 25.8 us; the launch traced here: 25.7 us
  Pallas kernels  24.2 us (94%)
  local copies, waits for them, and re-layouts  1.47 us (6%)
    pallas_call x1, Pallas kernels, on_device(): pl.pallas_call(functools.partial(kernel, (depth, rows, lanes, doses, slab...  24.2 us
    unnamed x1, local copies, waits for them, and re-layouts  1.47 us

profile of v3, /device:TPU:0, one launch (start us, length us, event | category | flops | bytes accessed | tf_op | source)
XLA Modules:
  0.0 25.7 jit_solution(13246891095317450683)
XLA Ops:
  0.0 24.2 %bake_adjoint.1 = f32[128,128]{1,0:T(8,128)} custom-call(f32[256,128]{1,0:T(8,128)} %bitcast.6, f32[256,128]{1,0:T(8,128)} %bitcast.7, f32[2,256,128]{2,1,0:T(8,128)} %bitcast.5, f32[16]{0:T(128)} %levels_in.1, s32[2]{0:T(128)} %index_in.1), custom_call_target="tpu_custom_call" | custom-call | tf_op jit(solution)/shard_map/bake_adjoint/pallas_call | solution.py:325
  24.2 1.5 %copy.7 = f32[16,8,128]{2,1,0:T(8,128)} copy(f32[16,8,128]{2,1,0:T(8,128)} %bitcast.4) | data formatting | bytes 131072

commit v4 on v3

--- a/solution.py
+++ b/solution.py
@@ -142,7 +142,7 @@
             body(jnp.where(j < skip_low, j, j + gap) if gap else j)
             return carry
 
-        lax.fori_loop(0, count, step, 0)
+        lax.fori_loop(0, count, step, 0, unroll=2)
 
     def expose(h):
         def body(j):

time: 25.8 us -> 23.8 us (0.922)
  Pallas kernels: 24.2 us -> 22.2 us
    pallas_call x1, Pallas kernels: 24.2 us -> 22.2 us  [on_device(): pl.pallas_call(functools.partial(kernel, (depth, rows, lanes, doses, slab...]
where the time goes in v4:
time: 23.8 us; the launch traced here: 23.7 us
  Pallas kernels  22.2 us (93%)
  local copies, waits for them, and re-layouts  1.47 us (6%)
    pallas_call x1, Pallas kernels, on_device(): pl.pallas_call(functools.partial(kernel, (depth, rows, lanes, doses, slab...  22.2 us
    unnamed x1, local copies, waits for them, and re-layouts  1.47 us

profile of v4, /device:TPU:0, one launch (start us, length us, event | category | flops | bytes accessed | tf_op | source)
XLA Modules:
  0.0 23.7 jit_solution(10506922876624293582)
XLA Ops:
  0.0 22.2 %bake_adjoint.1 = f32[128,128]{1,0:T(8,128)} custom-call(f32[256,128]{1,0:T(8,128)} %bitcast.6, f32[256,128]{1,0:T(8,128)} %bitcast.7, f32[2,256,128]{2,1,0:T(8,128)} %bitcast.5, f32[16]{0:T(128)} %levels_in.1, s32[2]{0:T(128)} %index_in.1), custom_call_target="tpu_custom_call" | custom-call | tf_op jit(solution)/shard_map/bake_adjoint/pallas_call | solution.py:325
  22.2 1.5 %copy.7 = f32[16,8,128]{2,1,0:T(8,128)} copy(f32[16,8,128]{2,1,0:T(8,128)} %bitcast.4) | data formatting | bytes 131072

commit v5 on v4

--- a/solution.py
+++ b/solution.py
@@ -73,11 +73,12 @@
             send(ref.at[0, pl.ds(first, width)], ref.at[0, pl.ds(last, width)], {"tx": before}),
         ]
 
-    def pass_rims(ref, width):
-        return [
-            send(ref.at[0, pl.ds(first - width, width)], ref.at[1, pl.ds(first - width, width)], {"ty": away}),
-            send(ref.at[0, pl.ds(last, width)], ref.at[1, pl.ds(last, width)], {"ty": away}),
-        ]
+    def pass_rims(rims, ref, width):
+        passed = []
+        for copy, start in zip(rims, (first - width, last)):
+            copy.wait_recv()
+            passed.append(send(ref.at[0, pl.ds(start, width)], ref.at[1, pl.ds(start, width)], {"ty": away}))
+        return passed
 
     def clear(ref, *places):
         for j in places:
@@ -142,7 +143,8 @@
             body(jnp.where(j < skip_low, j, j + gap) if gap else j)
             return carry
 
-        lax.fori_loop(0, count, step, 0, unroll=2)
+        unroll = next(n for n in (4, 3, 2, 1) if count % n == 0)
+        lax.fori_loop(0, count, step, 0, unroll=unroll)
 
     def expose(h):
         def body(j):
@@ -225,12 +227,8 @@
     each_row(expose(1), first, last)
     que_half.wait_recv()
     each_row(forward0, first + 1, last - 1)
-    for copy in img_rims:
-        copy.wait_recv()
-    img_pass = pass_rims(img, IMG)
-    for copy in que_rims:
-        copy.wait_recv()
-    que_pass = pass_rims(que, QUE)
+    img_pass = pass_rims(img_rims, img, IMG)
+    que_pass = pass_rims(que_rims, que, QUE)
     each_row(forward1, first + 2, last - 2)
     each_row(forward2, first + 3, last - 3)
     each_row(expose(0), first - 3, last + 3, first, last)
@@ -256,42 +254,37 @@
         for j, inner in ((first - 2, first - 1), (last + 1, last)):
             b1a[h, j] = acid_lateral * b2a[h, inner]
 
-    middle = rows // 2
-    chunks = (pl.ds(0, first + middle), pl.ds(first + middle, last + IMG - first - middle))
-    halves = []
-    for side, (edge, inner, outside, inside) in enumerate(
-        (
-            (first - 3, first - 2, (first - 2, first), (first, first + middle)),
-            (last + 2, last + 1, (last, last + 2), (first + middle, last)),
-        )
-    ):
+    middle = first + rows // 2
+    chunks = [pl.ds(first - IMG, IMG), pl.ds(last, IMG), pl.ds(first, middle - first), pl.ds(middle, last - middle)]
+
+    def swap(chunk):
+        return send(part.at[1, chunk], half_sum.at[chunk], {"ty": away})
+
+    for edge, inner in ((first - 3, first - 2), (last + 2, last + 1)):
         for h in range(2):
             finish(h, edge, acid_lateral * b1a[h, inner])
-        each_row(functools.partial(back0, own_row=False), *outside)
-        each_row(back0, *inside)
-        halves.append(send(part.at[1, chunks[side]], half_sum.at[chunks[side]], {"ty": away}))
+    each_row(functools.partial(back0, own_row=False), first - 2, last + 2, first, last)
+    halves = [swap(chunks[0]), swap(chunks[1])]
+    each_row(back0, first, middle)
+    halves.append(swap(chunks[2]))
+    each_row(back0, middle, last)
+    halves.append(swap(chunks[3]))
 
     def layers(k):
         return pl.ds(pl.multiple_of(peers[k] * slab, slab), slab)
 
     sums = []
-    for side in range(2):
-        halves[side].wait_recv()
-        half_sum[chunks[side]] += part[0, chunks[side]]
-        reach, beside, there = (
-            (pl.ds(first - IMG, IMG), before, got_high) if side == 0 else (pl.ds(last, IMG), after, got_low)
-        )
-        for k in range(doses):
-            sums.append(send(half_sum.at[reach, layers(k)], there.at[k], {"tx": beside, "dose": peers[k]}))
-        start, count = (0, middle) if side == 0 else (middle, rows - middle)
-        for k in range(1, doses):
-            sums.append(
-                send(
-                    half_sum.at[pl.ds(first + start, count), layers(k)],
-                    got.at[k, pl.ds(start, count)],
-                    {"dose": peers[k]},
-                )
-            )
+    for half, chunk, target in zip(halves, chunks, ((before, got_high), (after, got_low), None, None)):
+        half.wait_recv()
+        half_sum[chunk] += part[0, chunk]
+        if target:
+            for k in reversed(range(doses)):
+                there = {"tx": target[0], "dose": peers[k]}
+                sums.append(send(half_sum.at[chunk, layers(k)], target[1].at[k], there))
+        else:
+            inside = pl.ds(chunk.start - first, chunk.size)
+            for k in range(1, doses):
+                sums.append(send(half_sum.at[chunk, layers(k)], got.at[k, inside], {"dose": peers[k]}))
     for copy in sums:
         copy.wait_recv()
     for r in range(rows):
@@ -319,7 +312,7 @@
     flat = (depth * rows, lanes)
     turned = (wide, depth // 8, 8, lanes)
     field = pltpu.VMEM((2,) + turned, jnp.float32)
-    copies = 11 + 2 + 2 * (doses - 1) + 2 * doses
+    copies = 11 + 4 + 2 * (doses - 1) + 2 * doses
     vmem = pl.BlockSpec(memory_space=pltpu.VMEM)
     anywhere = pl.BlockSpec(memory_space=pl.ANY)
     out = pl.pallas_call(

time: 23.8 us -> 22.8 us (0.958)
  Pallas kernels: 22.2 us -> 21.2 us
    pallas_call x1, Pallas kernels: 22.2 us -> 21.2 us  [on_device(): pl.pallas_call(functools.partial(kernel, (depth, rows, lanes, doses, slab...]
where the time goes in v5:
time: 22.8 us; the launch traced here: 22.6 us
  Pallas kernels  21.2 us (93%)
  local copies, waits for them, and re-layouts  1.47 us (6%)
    pallas_call x1, Pallas kernels, on_device(): pl.pallas_call(functools.partial(kernel, (depth, rows, lanes, doses, slab...  21.2 us
    unnamed x1, local copies, waits for them, and re-layouts  1.47 us

profile of v5, /device:TPU:0, one launch (start us, length us, event | category | flops | bytes accessed | tf_op | source)
XLA Modules:
  0.0 22.6 jit_solution(4486454723232291704)
XLA Ops:
  0.0 21.2 %bake_adjoint.1 = f32[128,128]{1,0:T(8,128)} custom-call(f32[256,128]{1,0:T(8,128)} %bitcast.6, f32[256,128]{1,0:T(8,128)} %bitcast.7, f32[2,256,128]{2,1,0:T(8,128)} %bitcast.5, f32[16]{0:T(128)} %levels_in.1, s32[2]{0:T(128)} %index_in.1), custom_call_target="tpu_custom_call" | custom-call | tf_op jit(solution)/shard_map/bake_adjoint/pallas_call | solution.py:318
  21.2 1.5 %copy.7 = f32[16,8,128]{2,1,0:T(8,128)} copy(f32[16,8,128]{2,1,0:T(8,128)} %bitcast.4) | data formatting | bytes 131072
